TPU v7x, 32 devices: a whole 2x2x4 slice. The times are simulated.
32 devices in a mesh: tm: 8 (over z, core), lon: 2 (over y), ens: 2 (over x).
Axes of the slice: x: 2, y: 2, z: 4, core: 2. Of those that a mesh axis runs over, the one named last changes fastest.
Arguments:
- anomalies: bfloat16 [2048, 1024], P('lon', 'ens'), may hold values from -6 to 6
- localization: bfloat16 [16, 3, 128, 128], P('lon'), may hold values from -0.3125 to 0.3125
- innovations: float32 [8, 1024], P('tm', 'lon'), may hold values from -6 to 6
- obs_cell: int32 [8, 1024], P('tm', 'lon'), may hold values from 0 to 1023
- tangent_blocks: float32 [8, 8, 128, 128], P('tm'), may hold values from -1 to 2
- tangent_order: int32 [8, 8], P('tm'), may hold values from 0 to 7, each once within a row
Outputs:
- forward_states: float32 [8, 1024, 1024], P('tm', ('ens', 'lon'))
- adjoint_states: float32 [8, 1024, 1024], P('tm', ('ens', 'lon'))
Inputs may be any that keep to these rules, and one draw needn't show every extreme that they name: Observation j of a step lies in sector j // 512, at that sector's cell obs_cell. `tangent_order`: each step's row names every block index once.
All inputs are finite; a program needn't handle non-finite values.
Results may differ from a plain program's by a relative error of at most 0.015.
Values may be sent and summed in bfloat16 or wider, within the bound.
A program may use at most 64 MiB of HBM per device.

v0:
```python
import jax
import jax.numpy as jnp
from jax import lax
from jax.sharding import PartitionSpec as P

BLK = 128


precise_mode = lax.Precision.HIGHEST


def extended(cells, sides, width):
    for axis, dim in sides:
        count = lax.axis_size(axis)
        head = lax.slice_in_dim(cells, 0, width, axis=dim)
        tail = lax.slice_in_dim(cells, cells.shape[dim] - width, cells.shape[dim], axis=dim)
        cells = jnp.concatenate(
            [
                lax.ppermute(tail, axis, [(i, (i + 1) % count) for i in range(count)]),
                cells,
                lax.ppermute(head, axis, [((i + 1) % count, i) for i in range(count)]),
            ],
            axis=dim,
        )
    return cells


def entering(array, axis, join, neutral, backward):
    count = lax.axis_size(axis)
    place = lax.axis_index(axis)
    ahead = count - 1 - place if backward else place
    gathered = jax.tree.map(
        lambda a, kind: lax.all_gather(a.astype(kind), axis),
        array,
        jax.tree.map(lambda a: jnp.bfloat16 if a.dtype == jnp.float32 else a.dtype, array),
    )
    state = jax.tree.map(lambda a, e: jnp.zeros_like(a) + jnp.asarray(e, a.dtype), array, neutral)

    def one(turn, state):
        source = count - 1 - turn if backward else turn
        return join(
            state,
            jax.tree.map(
                lambda a, own: lax.dynamic_index_in_dim(a, source, 0, False).astype(own.dtype),
                gathered,
                array,
            ),
        )

    return lax.fori_loop(0, ahead, one, state)


def forward_apply(perm_matrix, blocks, state):
    row_count = state.shape[0]
    split_point = state.reshape(row_count, blocks.shape[0], blocks.shape[1])
    chosen = jnp.einsum("ik,mkc->mic", perm_matrix, split_point, precision=precise_mode)
    return jnp.einsum("mic,idc->mid", chosen, blocks, precision=precise_mode).reshape(row_count, -1)


def adjoint_apply(perm_matrix, blocks, state):
    row_count = state.shape[0]
    split_point = state.reshape(row_count, blocks.shape[0], blocks.shape[1])
    moved = jnp.einsum("mic,icd->mid", split_point, blocks, precision=precise_mode)
    placed = jnp.einsum("ij,mid->mjd", perm_matrix, moved, precision=precise_mode)
    return placed.reshape(row_count, -1)


def operator_product(left_perm, left_blocks, right_perm, right_blocks):
    perm_matrix = jnp.dot(left_perm, right_perm, precision=precise_mode)
    picked = jnp.einsum("ik,kce->ice", left_perm, right_blocks, precision=precise_mode)
    blocks = jnp.einsum("icd,ide->ice", left_blocks, picked, precision=precise_mode)
    return (perm_matrix, blocks)


def forward_combine(earlier, later):
    perm_matrix, blocks = operator_product(later[0], later[1], earlier[0], earlier[1])
    return (perm_matrix, blocks, forward_apply(later[0], later[1], earlier[2]) + later[2])


def adjoint_combine(earlier, later):
    perm_matrix, blocks = operator_product(earlier[0], earlier[1], later[0], later[1])
    return (perm_matrix, blocks, adjoint_apply(later[0], later[1], earlier[2]) + later[2])


def on_device(anomalies, localization, innovations, obs_cell, tangent_blocks, tangent_order):
    cells = anomalies.shape[0]
    half_cols = anomalies.shape[1]
    sector_count = lax.axis_size("lon")
    steps_here = tangent_blocks.shape[0]
    block_count = tangent_blocks.shape[1]
    block_size = tangent_blocks.shape[2]
    full_anomalies = lax.all_gather(anomalies, "ens", axis=1, tiled=True)
    positions = lax.broadcasted_iota(jnp.int32, (1, 1, cells), 2)
    obs_onehot = (obs_cell[:, :, None] == positions).astype(jnp.float32)
    cell_weight = jnp.einsum("to,toc->ct", innovations, obs_onehot, precision=precise_mode)
    weighted = (
        jnp.transpose(cell_weight)[:, :, None] * anomalies[None].astype(jnp.float32)
    ).astype(jnp.bfloat16)
    padded = extended(weighted, (("lon", 1),), BLK)
    cell_blocks = cells // BLK
    stacked = padded.reshape(steps_here, cell_blocks + 2, BLK, half_cols)
    localized = jnp.zeros((steps_here, cell_blocks, BLK, half_cols), jnp.float32)
    for offset in range(3):
        localized = localized + jnp.einsum(
            "bij,tbjm->tbim",
            localization[:, offset],
            stacked[:, offset : offset + cell_blocks],
            preferred_element_type=jnp.float32,
        )
    localized = localized.reshape(steps_here, cells, half_cols).astype(jnp.bfloat16)
    scale = float(cells * sector_count) ** (-0.5)
    forcing = lax.psum_scatter(
        (
            jnp.einsum("tcm,cr->mtr", localized, full_anomalies, preferred_element_type=jnp.float32)
            * scale
        ).astype(jnp.bfloat16),
        "lon",
        scatter_dimension=0,
        tiled=True,
    ).astype(jnp.float32)
    block_ids = lax.broadcasted_iota(jnp.int32, (1, 1, block_count), 2)
    perm_all = (tangent_order[:, :, None] == block_ids).astype(jnp.float32)
    forward_items = (perm_all[0], tangent_blocks[0], forcing[:, 0])
    adjoint_items = [
        (
            perm_all[0],
            tangent_blocks[0],
            adjoint_apply(perm_all[0], tangent_blocks[0], forcing[:, 0]),
        )
    ]
    adjoint_total = adjoint_items[steps_here - 1]
    empty = jnp.zeros((forcing.shape[0], forcing.shape[2]), jnp.float32)
    identity = (
        jnp.eye(block_count, dtype=jnp.float32),
        jnp.broadcast_to(
            jnp.eye(block_size, dtype=jnp.float32), (block_count, block_size, block_size)
        ),
        empty,
    )
    start_state = entering(forward_items, "tm", forward_combine, identity, False)[2]
    end_adjoint = entering(adjoint_total, "tm", adjoint_combine, identity, True)[2]
    state = start_state
    index = 0
    state = forward_apply(perm_all[index], tangent_blocks[index], state) + forcing[:, index]
    forward_list = [state]
    adjoint = end_adjoint
    adjoint_list = [empty] * steps_here
    index = 0
    adjoint = adjoint_apply(perm_all[index], tangent_blocks[index], adjoint + forcing[:, index])
    adjoint_list[index] = adjoint
    return (jnp.stack(forward_list, axis=0), jnp.stack(adjoint_list, axis=0))


def solution(mesh):
    placed = (
        P("lon", "ens"),
        P("lon", None, None, None),
        P("tm", "lon"),
        P("tm", "lon"),
        P("tm", None, None, None),
        P("tm", None),
    )
    return jax.shard_map(
        on_device,
        mesh=mesh,
        in_specs=placed,
        out_specs=(P("tm", ("ens", "lon"), None), P("tm", ("ens", "lon"), None)),
        check_vma=False,
    )
```

profile of v0, /device:TPU:0, one launch (start us, length us, event | category | flops | bytes accessed | tf_op | source)
XLA Modules:
  0.0 218.8 jit_solution(14471709543337862312)
XLA Ops:
  8.8 1.5 fusion.18
  10.6 3.0 %collective-permute-start.1 = (bf16[1,128,512]{2,1,0:T(8,128)(2,1)S(1)}, bf16[1,128,512]{2,1,0:T(8,128)(2,1)S(1)}, u32[]{:S(2)}, u32[]{:S(2)}) collective-permute-start(bf16[1,128,512]{2,1,0:T(8,128)(2,1)S(1)} %get-tuple-element.210), channel_id=1, source_target_pairs={{2,0},{0,2},{3,1},{1,3},{6,4},{4,6},{7,5},{5,7},{10,8},{8,10},{11,... | collective-permute-start | bytes 393224 | tf_op jit(solution)/shard_map/ppermute | solution.py:21
  13.8 4.2 %collective-permute-done.1 = bf16[1,128,512]{2,1,0:T(8,128)(2,1)S(1)} collective-permute-done((bf16[1,128,512]{2,1,0:T(8,128)(2,1)S(1)}, bf16[1,128,512]{2,1,0:T(8,128)(2,1)S(1)}, u32[]{:S(2)}, u32[]{:S(2)}) %collective-permute-start.1) | collective-permute-done | bytes 131104 | tf_op jit(solution)/shard_map/ppermute | solution.py:21
  18.0 2.0 collective-permute-done
  21.4 24.9 %all-gather.7.cloned.1.call-done = bf16[1024,1024]{1,0:T(8,128)(2,1)} async-done(((bf16[1024,512]{1,0:T(8,128)(2,1)}), bf16[1024,1024]{1,0:T(8,128)(2,1)}) %all-gather.7.cloned.1.call-update) | async-done | bytes 2097168 | tf_op jit(solution)/shard_map/all_gather | solution.py:92
  46.2 3.9 %fusion.20 = bf16[512,1,1024]{2,0,1:T(8,128)(2,1)} fusion(bf16[1024,512]{1,0:T(8,128)(2,1)S(1)} %bitcast.189, bf16[1024,1024]{1,0:T(8,128)(2,1)} %all-gather.7.cloned.1.call-done), kind=kOutput, calls=%fused_computation.30 | convolution fusion | flops 1074790400 | bytes 4194304 | tf_op jit(solution)/shard_map/tcm,cr->mtr/dot_general | solution.py:114
  51.1 19.6 %reduce-scatter.2.cloned.1.call-done = bf16[256,1,1024]{2,0,1:T(8,128)(2,1)} async-done(((bf16[512,1,1024]{2,0,1:T(8,128)(2,1)}), bf16[256,1,1024]{2,0,1:T(8,128)(2,1)}) %reduce-scatter.2.cloned.1.call-update) | async-done | bytes 524304 | tf_op jit(solution)/shard_map/reduce_scatter | solution.py:112
  70.7 1.9 fusion.22
  72.6 1.1 copy.51
  74.4 1.2 fusion.23
  76.7 12.8 %all_gather.11 = bf16[8,8,8]{2,1,0:T(8,128)(2,1)S(1)} all-gather(bf16[1,8,8]{2,1,0:T(8,128)(2,1)S(1)} %convert_convert_fusion), channel_id=1, replica_groups=mesh['tm'=8,'lon'=2,'ens'=2] {'tm'}, dimensions={0}, use_global_device_ids=true | all-gather | bytes 1152 | tf_op jit(solution)/shard_map/all_gather | solution.py:33
  89.4 40.9 %all-gather.9.cloned.1.call-done = bf16[8,256,1024]{2,1,0:T(8,128)(2,1)} async-done(((bf16[1,256,1024]{2,1,0:T(8,128)(2,1)}), bf16[8,256,1024]{2,1,0:T(8,128)(2,1)}) %all-gather.9.cloned.1.call-update) | async-done | bytes 4194320 | tf_op jit(solution)/shard_map/all_gather | solution.py:33
  131.4 1.2 fusion.33
  132.6 1.3 copy.42
  133.9 43.5 %all-gather.11.cloned.1.call-done = bf16[8,256,1024]{2,1,0:T(8,128)(2,1)} async-done(((bf16[1,256,1024]{2,1,0:T(8,128)(2,1)}), bf16[8,256,1024]{2,1,0:T(8,128)(2,1)}) %all-gather.11.cloned.1.call-update) | async-done | bytes 4194320 | tf_op jit(solution)/shard_map/all_gather | solution.py:33
  177.6 28.7 %while.29 = (s32[]{:T(128)}, f32[256,1024]{1,0:T(8,128)S(1)}, s32[]{:T(128)}, bf16[8,8,128,128]{3,2,1,0:T(8,128)(2,1)}, bf16[8,8,8]{2,1,0:T(8,128)(2,1)S(1)}, /*...) while((s32[]{:T(128)}, f32[256,1024]{1,0:T(8,128)S(1)}, s32[]{:T(128)}, ...), condition=%wide.region_4.5_spmd, body=%wide.region_3.4_spmd.sunk | while | flops 428343296 | bytes 9177255 | solution.py:50
  177.8 1.6 convolution_bitcast_fusion.9
  180.5 1.4 bitcast_add_fusion.2
  181.9 1.6 convolution_bitcast_fusion.9
  184.5 1.4 bitcast_add_fusion.2
  185.9 1.6 convolution_bitcast_fusion.9
  188.6 1.4 bitcast_add_fusion.2
  190.0 1.6 convolution_bitcast_fusion.9
  192.7 1.4 bitcast_add_fusion.2
  194.1 1.6 convolution_bitcast_fusion.9
  196.8 1.4 bitcast_add_fusion.2
  198.1 1.6 convolution_bitcast_fusion.9
  200.8 1.4 bitcast_add_fusion.2
  202.2 1.6 convolution_bitcast_fusion.9
  204.9 1.4 bitcast_add_fusion.2
  206.3 1.1 convolution_bitcast_fusion.5
  207.4 1.2 convolution_bitcast_fusion.2
  (57 shorter events, 16.3 us)
Async XLA Ops:
  8.0 0.8 copy-start
  8.0 2.3 %copy-start.3 = (bf16[1024,512]{1,0:T(8,128)(2,1)S(1)}, bf16[1024,512]{1,0:T(8,128)(2,1)}, u32[]{:S(2)}) copy-start(bf16[1024,512]{1,0:T(8,128)(2,1)} %param.10) | copy-start | bytes 3145732
  8.0 38.2 %all-gather.7.cloned.1.call-start = ((), (), s32[]{:S(2)}) async-start(), calls=%async_computation.2 | async-start | bytes 3145728 | tf_op jit(solution)/shard_map/all_gather | solution.py:92
  8.8 61.9 %reduce-scatter.2.cloned.1.call-start = ((), (), s32[]{:S(2)}) async-start(), calls=%async_computation.3 | async-start | bytes 1572864 | tf_op jit(solution)/shard_map/reduce_scatter | solution.py:112
  10.6 9.5 %copy-start.5 = (bf16[8,3,128,128]{3,2,1,0:T(8,128)(2,1)S(1)}, bf16[8,3,128,128]{3,2,1,0:T(8,128)(2,1)}, u32[]{:S(2)}) copy-start(bf16[8,3,128,128]{3,2,1,0:T(8,128)(2,1)} %param.11) | copy-start | bytes 2359300
  10.6 7.4 %collective-permute-start.1 = (bf16[1,128,512]{2,1,0:T(8,128)(2,1)S(1)}, bf16[1,128,512]{2,1,0:T(8,128)(2,1)S(1)}, u32[]{:S(2)}, u32[]{:S(2)}) collective-permute-start(bf16[1,128,512]{2,1,0:T(8,128)(2,1)S(1)} %get-tuple-element.210), channel_id=1, source_target_pairs={{2,0},{0,2},{3,1},{1,3},{6,4},{4,6},{7,5},{5,7},{10,8},{8,10},{11,... | collective-permute-start | bytes 393224 | tf_op jit(solution)/shard_map/ppermute | solution.py:21
  13.7 6.3 %collective-permute-start = (bf16[1,128,512]{2,1,0:T(8,128)(2,1)S(1)}, bf16[1,128,512]{2,1,0:T(8,128)(2,1)S(1)}, u32[]{:S(2)}, u32[]{:S(2)}) collective-permute-start(bf16[1,128,512]{2,1,0:T(8,128)(2,1)S(1)} %get-tuple-element.209), channel_id=1, source_target_pairs={{0,2},{2,0},{1,3},{3,1},{4,6},{6,4},{5,7},{7,5},{8,10},{10,8},{9,1... | collective-permute-start | bytes 393224 | tf_op jit(solution)/shard_map/ppermute | solution.py:19
  46.2 4.0 %copy-start.1 = (f32[1,8,128,128]{3,2,1,0:T(8,128)S(1)}, f32[1,8,128,128]{3,2,1,0:T(8,128)}, u32[]{:S(2)}) copy-start(f32[1,8,128,128]{3,2,1,0:T(8,128)} %param.14) | copy-start | bytes 1572868
  50.2 39.2 %all-gather.5.cloned.1.call-start = ((), (), s32[]{:S(2)}) async-start(), calls=%async_computation.1 | async-start | bytes 2359296 | tf_op jit(solution)/shard_map/all_gather | solution.py:33
  51.0 79.3 %all-gather.9.cloned.1.call-start = ((), (), s32[]{:S(2)}) async-start(), calls=%async_computation.4 | async-start | bytes 4718592 | tf_op jit(solution)/shard_map/all_gather | solution.py:33
  72.5 1.8 copy-start.6
  72.6 104.9 %all-gather.11.cloned.1.call-start = ((), (), s32[]{:S(2)}) async-start(), calls=%async_computation.5 | async-start | bytes 4718592 | tf_op jit(solution)/shard_map/all_gather | solution.py:33
  177.6 28.7 %copy-start.2 = (bf16[256,1,1024]{2,0,1:T(8,128)(2,1)S(1)}, bf16[256,1,1024]{2,0,1:T(8,128)(2,1)}, u32[]{:S(2)}) copy-start(bf16[256,1,1024]{2,0,1:T(8,128)(2,1)} %reduce-scatter.2.cloned.1.call-done) | copy-start | bytes 1572868
  208.6 1.6 copy-start.4
Sparse Core Ops, SparseCore 0:
  10.4 35.7 all-gather.6
  50.3 20.3 reduce-scatter.1
Sparse Core Ops, SparseCore 1:
  52.8 29.0 all-gather.4
  84.0 46.2 all-gather.8
  131.8 45.5 all-gather.10
where the time goes:
time: 220 us; the launch traced here: 219 us
  waiting for transfers between devices  136 us (62%)
  matrix products  28.4 us (13%)
  between operations  15.9 us (7%)
  other arithmetic  13.7 us (6%)
  blocking collectives  12.8 us (6%)
  local copies, waits for them, and re-layouts  8.49 us (4%)
  starting transfers between devices  3.32 us (2%)
    all_gather x3, waiting for transfers between devices, entering(): lax.all_gather(a.astype(kind), axis)  84.4 us
    all_gather x1, waiting for transfers between devices, on_device(): full_anomalies = lax.all_gather(anomalies, 'ens', axis=1, tiled=True)  24.9 us
    reduce_scatter x1, waiting for transfers between devices, on_device(): lax.psum_scatter((jnp.einsum('tcm,cr->mtr', localized, full_anomalies, pr...  19.6 us
    dot_general x9, matrix products, adjoint_apply(): jnp.einsum('mic,icd->mid', split_point, blocks, precision=precise_mode)  13.1 us
    all_gather x1, blocking collectives, entering(): lax.all_gather(a.astype(kind), axis)  12.8 us
    add x7, other arithmetic, adjoint_combine(): adjoint_apply(later[0], later[1], earlier[2]) + later[2]  9.49 us
    dot_general x9, matrix products, adjoint_apply(): jnp.einsum('ij,mid->mjd', perm_matrix, moved, precision=precise_mode)  6.82 us
  transfers between devices with their start and end apart: 7, of which 6 were waited for; matrix products, arithmetic and copies ran while one was open for 6% of the time, Pallas kernels for 0%

commit v1 on v0

v1 whole, which is shorter than its diff:
```python
import functools

import jax
import jax.numpy as jnp
from jax import lax
from jax.experimental import pallas as pl
from jax.experimental.pallas import tpu as pltpu
from jax.sharding import PartitionSpec as P

BLK = 128
SUBS = 4
F32 = jnp.float32
BF16 = jnp.bfloat16


def mm(a, b):
    return jnp.dot(a, b, preferred_element_type=F32)


def weight_column(innov, cells_of, first):
    ids = first + lax.broadcasted_iota(jnp.int32, (BLK, innov.shape[1]), 0)
    return jnp.sum(jnp.where(cells_of == ids, innov, 0.0), axis=1, keepdims=True)


def kernel(
    dims,
    anom,
    local,
    innov,
    obs,
    tangent,
    order,
    fwd_out,
    adj_out,
    other,
    halo,
    halo_innov,
    halo_obs,
    weighted,
    loc_t,
    part_send,
    part_recv,
    part_own,
    force,
    force_a,
    f_in,
    f_out,
    a_in,
    a_out,
    f_now,
    a_now,
    map_f,
    map_a,
    x_send,
    x_recv,
    xf_send,
    xf_recv,
    h_send,
    h_recv,
    o_send,
    o_recv,
    r_send,
    r_recv,
    f_send,
    f_recv,
    a_send,
    a_recv,
):
    n_tm, n_lon, n_ens, rows, chunk = dims
    cells, cols = anom.shape
    n_blocks = cells // BLK
    n_pieces = tangent.shape[1]
    n_chunks = rows // chunk
    group = cols // BLK
    t, l, e = lax.axis_index("tm"), lax.axis_index("lon"), lax.axis_index("ens")
    parity = lax.rem(t, 2)
    mate = t + 1 - 2 * parity
    right, left = lax.rem(l + 1, n_lon), lax.rem(l + n_lon - 1, n_lon)

    def remote(src, dst, send, recv, where):
        return pltpu.make_async_remote_copy(
            src_ref=src,
            dst_ref=dst,
            send_sem=send,
            recv_sem=recv,
            device_id=where,
            device_id_type=pl.DeviceIdType.MESH,
        )

    def at(tt=None, ll=None, ee=None):
        return (t if tt is None else tt, l if ll is None else ll, e if ee is None else ee)

    barrier = pltpu.get_barrier_semaphore()

    def greet(where):
        pl.semaphore_signal(
            barrier, inc=1, device_id=where, device_id_type=pl.DeviceIdType.MESH
        )

    for d in range(1, n_ens):
        greet(at(ee=lax.rem(e + d, n_ens)))
    for d in range(1, n_lon):
        greet(at(ll=lax.rem(l + d, n_lon)))

    @pl.when(t > 0)
    def _():
        greet(at(tt=t - 1))

    @pl.when(t < n_tm - 1)
    def _():
        greet(at(tt=t + 1))

    ends = (t > 0).astype(jnp.int32) + (t < n_tm - 1).astype(jnp.int32)
    pl.semaphore_wait(barrier, n_ens - 1 + n_lon - 1 + ends)

    half = cells // 2
    sub = half // SUBS

    def x_copy(d, s, send, recv, where, source):
        span = pl.ds(pl.multiple_of(parity * half + s * sub, sub), sub)
        return remote(source.at[span], other.at[d - 1, span], send.at[d - 1, s], recv.at[d - 1, s], where)

    edge = pl.ds(pl.multiple_of((1 - parity) * (cells - BLK), BLK), BLK)
    toward = jnp.where(parity == 0, right, left)
    halo_copy = remote(anom.at[edge], halo.at[parity], h_send.at[0], h_recv.at[0], at(ll=toward))
    halo_copy.start()
    obs_copies = []
    for side, where in ((0, right), (1, left)):
        obs_copies.append(
            remote(innov, halo_innov.at[side], o_send.at[side], o_recv.at[side], at(ll=where))
        )
        obs_copies.append(
            remote(obs, halo_obs.at[side], o_send.at[2 + side], o_recv.at[2 + side], at(ll=where))
        )
    for copy in obs_copies:
        copy.start()
    x_copies = [
        [
            x_copy(d, s, x_send, x_recv, at(ee=lax.rem(e + d, n_ens)), anom)
            for s in range(SUBS)
        ]
        for d in range(1, n_ens)
    ]
    for s in range(SUBS):
        for d in range(1, n_ens):
            x_copies[d - 1][s].start()

    innov_row, obs_row = innov[...], obs[...]

    def weigh(b, _):
        start = pl.multiple_of(b * BLK, BLK)
        column = weight_column(innov_row, obs_row, start)
        value = column * anom[pl.ds(start, BLK), :].astype(F32)
        weighted[pl.ds(pl.multiple_of(start + BLK, BLK), BLK), :] = value.astype(BF16)
        return 0

    lax.fori_loop(0, n_blocks, weigh, 0)

    def localize(b):
        start = pl.multiple_of(b * BLK, BLK)
        ops = jnp.concatenate([local[b, 0], local[b, 1], local[b, 2]], axis=1)
        value = mm(ops, weighted[pl.ds(start, 3 * BLK), :])
        loc_t[:, pl.ds(start, BLK)] = value.T.astype(BF16)

    def inner(b, _):
        localize(b)
        return 0

    lax.fori_loop(1, n_blocks - 1, inner, 0)

    halo_copy.wait_recv()
    halo_mate = remote(halo.at[parity], halo.at[parity], h_send.at[1], h_recv.at[1], at(tt=mate))
    halo_mate.start()

    def split_map(i, _):
        block = tangent[0, i]
        high = block.astype(BF16)
        low = (block - high.astype(F32)).astype(BF16)
        map_a[i, 0:BLK, :] = high
        map_a[i, BLK : 2 * BLK, :] = low
        turned = block.T
        high = turned.astype(BF16)
        map_f[i, 0:BLK, :] = high
        map_f[i, BLK : 2 * BLK, :] = (turned - high.astype(F32)).astype(BF16)
        return 0

    lax.fori_loop(0, n_pieces, split_map, 0)

    for copy in obs_copies:
        copy.wait_recv()
    remote(
        halo.at[1 - parity], halo.at[1 - parity], h_send.at[1], h_recv.at[1], at(tt=mate)
    ).wait_recv()
    for side, first, place in ((0, cells - BLK, 0), (1, 0, cells + BLK)):
        column = weight_column(halo_innov[side], halo_obs[side], first)
        weighted[place : place + BLK, :] = (column * halo[side].astype(F32)).astype(BF16)
    localize(0)
    localize(n_blocks - 1)

    scale = float(cells * n_lon) ** (-0.5)

    def r_copy(d, k, c):
        span = pl.ds(pl.multiple_of(c * chunk, chunk), chunk)
        return remote(
            part_send.at[d - 1, k, span],
            part_recv.at[d - 1, k, span],
            r_send.at[d - 1, k, c],
            r_recv.at[d - 1, k, c],
            at(ll=lax.rem(l + d, n_lon)),
        )

    def partials(k, source):
        for d in range(1, n_lon + 1):
            dest = lax.rem(l + d, n_lon)
            mine = loc_t[pl.ds(pl.multiple_of(dest * rows, rows), rows), :]
            value = (mm(mine, source[...]) * scale).astype(BF16)
            if d < n_lon:
                part_send[d - 1, k] = value
                for c in range(n_chunks):
                    r_copy(d, k, c).start()
            else:
                part_own[k] = value

    partials(0, anom)
    mate_copies = []
    for s in range(SUBS):
        for d in range(1, n_ens):
            x_copies[d - 1][s].wait_recv()
            copy = x_copy(d, s, xf_send, xf_recv, at(tt=mate), other.at[d - 1])
            copy.start()
            mate_copies.append(copy)
    for s in range(SUBS):
        for d in range(1, n_ens):
            span = pl.ds(pl.multiple_of((1 - parity) * half + s * sub, sub), sub)
            remote(
                other.at[d - 1, span],
                other.at[d - 1, span],
                xf_send.at[d - 1, s],
                xf_recv.at[d - 1, s],
                at(tt=mate),
            ).wait_recv()
    for k in range(1, n_ens):
        partials(k, other.at[k - 1])

    slots = [order[0, i] for i in range(n_pieces)]
    inverse = []
    for j in range(n_pieces):
        place = jnp.int32(0)
        for i in range(n_pieces):
            place = jnp.where(slots[i] == j, jnp.int32(i), place)
        inverse.append(place)

    @pl.when(t == 0)
    def _():
        f_in[...] = jnp.zeros_like(f_in)

    @pl.when(t == n_tm - 1)
    def _():
        a_in[...] = jnp.zeros_like(a_in)

    def f_copy(c):
        return remote(f_out.at[c], f_in.at[c], f_send.at[c], f_recv.at[c], at(tt=lax.rem(t + 1, n_tm)))

    def a_copy(c):
        return remote(
            a_out.at[c], a_in.at[c], a_send.at[c], a_recv.at[c], at(tt=lax.rem(t + n_tm - 1, n_tm))
        )

    def gather_force(c):
        span = pl.ds(pl.multiple_of(c * chunk, chunk), chunk)
        for k in range(n_ens):
            total = part_own[k, span, :].astype(F32)
            for d in range(1, n_lon):
                r_copy(d, k, c).wait_recv()
                total = total + part_recv[d - 1, k, span, :].astype(F32)
            base = lax.rem(e - k + n_ens, n_ens) * group
            for q in range(group):
                force[c, base + q] = total[:, q * BLK : (q + 1) * BLK]

    def forward_chunk(c):
        @pl.when(t > 0)
        def _():
            f_copy(c).wait_recv()

        span = pl.ds(pl.multiple_of(c * chunk, chunk), chunk)
        f_now[...] = f_in[c]
        for i in range(n_pieces):
            state = f_now[slots[i]]
            value = mm(jnp.concatenate([state, state], axis=1), map_f[i]) + force[c, i]
            f_out[c, i] = value.astype(BF16)
            fwd_out[0, span, i * BLK : (i + 1) * BLK] = value

        @pl.when(t < n_tm - 1)
        def _():
            f_copy(c).start()

    def apply_force(c):
        for j in range(n_pieces):
            value = force[c, inverse[j]]
            high = value.astype(BF16)
            low = (value - high.astype(F32)).astype(BF16)
            both = map_a[inverse[j]]
            force_a[c, j] = mm(jnp.concatenate([high, high], axis=1), both) + mm(low, both[0:BLK])

    def adjoint_chunk(c):
        @pl.when(t < n_tm - 1)
        def _():
            a_copy(c).wait_recv()

        span = pl.ds(pl.multiple_of(c * chunk, chunk), chunk)
        a_now[...] = a_in[c]
        for j in range(n_pieces):
            state = a_now[inverse[j]]
            value = mm(jnp.concatenate([state, state], axis=1), map_a[inverse[j]]) + force_a[c, j]
            a_out[c, j] = value.astype(BF16)
            adj_out[0, span, j * BLK : (j + 1) * BLK] = value

        @pl.when(t > 0)
        def _():
            a_copy(c).start()

    def turn(s, _):
        @pl.when(s < n_chunks)
        def _():
            gather_force(s)

        c_f = s - t

        @pl.when((c_f >= 0) & (c_f < n_chunks))
        def _():
            forward_chunk(c_f)

        @pl.when(s < n_chunks)
        def _():
            apply_force(s)

        c_a = s - (n_tm - 1 - t)

        @pl.when((c_a >= 0) & (c_a < n_chunks))
        def _():
            adjoint_chunk(c_a)

        return 0

    lax.fori_loop(0, n_tm - 1 + n_chunks, turn, 0)

    halo_copy.wait_send()
    halo_mate.wait_send()
    for copy in obs_copies + mate_copies:
        copy.wait_send()
    for d in range(1, n_ens):
        for s in range(SUBS):
            x_copies[d - 1][s].wait_send()
    for d in range(1, n_lon):
        for k in range(n_ens):
            for c in range(n_chunks):
                r_copy(d, k, c).wait_send()

    @pl.when(t < n_tm - 1)
    def _():
        for c in range(n_chunks):
            f_copy(c).wait_send()

    @pl.when(t > 0)
    def _():
        for c in range(n_chunks):
            a_copy(c).wait_send()


def on_device(mesh_dims, anomalies, localization, innovations, obs_cell, tangent_blocks, tangent_order):
    n_tm, n_lon, n_ens = mesh_dims
    cells, cols = anomalies.shape
    rank = cols * n_ens
    rows = cols // n_lon
    chunk = min(64, rows)
    n_chunks = rows // chunk
    pieces = tangent_blocks.shape[1]
    obs = innovations.shape[1]
    vmem = pltpu.VMEM
    dma = pltpu.SemaphoreType.DMA
    state = (n_chunks, pieces, chunk, BLK)
    parts = (max(n_lon - 1, 1), n_ens, rows, cols)
    r_sems = (max(n_lon - 1, 1), n_ens, n_chunks)
    x_sems = (max(n_ens - 1, 1), SUBS)
    in_vmem = pl.BlockSpec(memory_space=pltpu.VMEM)
    out = jax.ShapeDtypeStruct((1, rows, rank), F32)
    return pl.pallas_call(
        functools.partial(kernel, (n_tm, n_lon, n_ens, rows, chunk)),
        out_shape=(out, out),
        in_specs=[in_vmem] * 5 + [pl.BlockSpec(memory_space=pltpu.SMEM)],
        out_specs=(in_vmem, in_vmem),
        scratch_shapes=[
            vmem((max(n_ens - 1, 1), cells, cols), BF16),
            vmem((2, BLK, cols), BF16),
            vmem((2, 1, obs), F32),
            vmem((2, 1, obs), jnp.int32),
            vmem((cells + 2 * BLK, cols), BF16),
            vmem((cols, cells), BF16),
            vmem(parts, BF16),
            vmem(parts, BF16),
            vmem((n_ens, rows, cols), BF16),
            vmem(state, F32),
            vmem(state, F32),
            vmem(state, BF16),
            vmem(state, BF16),
            vmem(state, BF16),
            vmem(state, BF16),
            vmem((pieces, chunk, BLK), BF16),
            vmem((pieces, chunk, BLK), BF16),
            vmem((pieces, 2 * BLK, BLK), BF16),
            vmem((pieces, 2 * BLK, BLK), BF16),
            dma(x_sems),
            dma(x_sems),
            dma(x_sems),
            dma(x_sems),
            dma((2,)),
            dma((2,)),
            dma((4,)),
            dma((4,)),
            dma(r_sems),
            dma(r_sems),
            dma((n_chunks,)),
            dma((n_chunks,)),
            dma((n_chunks,)),
            dma((n_chunks,)),
        ],
        compiler_params=pltpu.CompilerParams(
            collective_id=0, has_side_effects=True, vmem_limit_bytes=40 * 1024 * 1024
        ),
    )(anomalies, localization, innovations, obs_cell, tangent_blocks, tangent_order)


def solution(mesh):
    placed = (
        P("lon", "ens"),
        P("lon", None, None, None),
        P("tm", "lon"),
        P("tm", "lon"),
        P("tm", None, None, None),
        P("tm", None),
    )
    mesh_dims = tuple(mesh.shape[name] for name in ("tm", "lon", "ens"))
    return jax.shard_map(
        functools.partial(on_device, mesh_dims),
        mesh=mesh,
        in_specs=placed,
        out_specs=(P("tm", ("ens", "lon"), None), P("tm", ("ens", "lon"), None)),
        check_vma=False,
    )
```

time: 220 us -> 57.2 us (0.26)
  waiting for transfers between devices: 136 us -> 0 us
  Pallas kernels: 0 us -> 48.9 us
  matrix products: 28.4 us -> 0 us
  between operations: 15.9 us -> 0.65 us
  other arithmetic: 13.7 us -> 0 us
  blocking collectives: 12.8 us -> 0 us
  starting transfers between devices: 3.32 us -> 0 us
    all_gather x4 -> x0, waiting for transfers between devices: 109 us -> none  [the longest x3 84.4 us: entering(): lax.all_gather(a.astype(kind), axis)]
    pallas_call x0 -> x1, Pallas kernels: none -> 48.9 us  [on_device(): pl.pallas_call(functools.partial(kernel, (n_tm, n_lon, n_ens, rows, chunk...]
    dot_general x25 -> x0, matrix products: 28.4 us -> none  [the longest x9 13.1 us: adjoint_apply(): jnp.einsum('mic,icd->mid', split_point, blocks, precision=precise_mode)]
    reduce_scatter x1 -> x0, waiting for transfers between devices: 19.6 us -> none  [on_device(): lax.psum_scatter((jnp.einsum('tcm,cr->mtr', localized, full_anomalies, pr...]
    all_gather x1 -> x0, blocking collectives: 12.8 us -> none  [entering(): lax.all_gather(a.astype(kind), axis)]
    add x8 -> x0, other arithmetic: 10.6 us -> none  [the longest x7 9.49 us: adjoint_combine(): adjoint_apply(later[0], later[1], earlier[2]) + later[2]]
    ppermute x2 -> x0, waiting for transfers between devices: 6.23 us -> none  [the longest x1 4.25 us: extended(): lax.ppermute(head, axis, [((i + 1) % count, i) for i in range(count)])]
    unnamed x15 -> x14, local copies, waits for them, and re-layouts: 1.59 us -> 7.35 us
  transfers between devices with their start and end apart: 7 -> 0, of which waited for: 6 -> 0; matrix products, arithmetic and copies ran while one was open for 6% -> 0% of each run, Pallas kernels for 0% -> 0%
where the time goes in v1:
time: 57.2 us; the launch traced here: 56.9 us
  Pallas kernels  48.9 us (85%)
  local copies, waits for them, and re-layouts  7.35 us (13%)
  between operations  0.65 us (1%)
    pallas_call x1, Pallas kernels, on_device(): pl.pallas_call(functools.partial(kernel, (n_tm, n_lon, n_ens, rows, chunk...  48.9 us
    unnamed x14, local copies, waits for them, and re-layouts  7.35 us

profile of v1, /device:TPU:0, one launch (start us, length us, event | category | flops | bytes accessed | tf_op | source)
XLA Modules:
  0.0 56.9 jit_solution(7169723444502551327)
XLA Ops:
  0.6 0.0 copy-start
  0.6 1.2 %copy-done = bf16[1024,512]{1,0:T(8,128)(2,1)S(1)} copy-done((bf16[1024,512]{1,0:T(8,128)(2,1)S(1)}, bf16[1024,512]{1,0:T(8,128)(2,1)}, u32[]{:S(2)}) %copy-start) | copy-done | bytes 1048600
  1.9 0.0 copy-start.1
  1.9 1.1 %copy-done.1 = bf16[8,3,128,128]{3,2,1,0:T(8,128)(2,1)S(1)} copy-done((bf16[8,3,128,128]{3,2,1,0:T(8,128)(2,1)S(1)}, bf16[8,3,128,128]{3,2,1,0:T(8,128)(2,1)}, u32[]{:S(2)}) %copy-start.1) | copy-done | bytes 786456
  3.0 0.0 copy-start.2
  3.0 1.0 %copy-done.2 = f32[1,8,128,128]{3,2,1,0:T(8,128)S(1)} copy-done((f32[1,8,128,128]{3,2,1,0:T(8,128)S(1)}, f32[1,8,128,128]{3,2,1,0:T(8,128)}, u32[]{:S(2)}) %copy-start.2) | copy-done | bytes 524312
  4.0 0.0 copy-start.3
  4.0 0.7 %copy-done.3 = f32[1,512]{1,0:T(1,128)S(1)} copy-done((f32[1,512]{1,0:T(1,128)S(1)}, f32[1,512]{1,0:T(1,128)}, u32[]{:S(2)}) %copy-start.3) | copy-done | bytes 2072
  4.7 0.0 copy-start.4
  4.7 0.7 %copy-done.4 = s32[1,512]{1,0:T(1,128)S(1)} copy-done((s32[1,512]{1,0:T(1,128)S(1)}, s32[1,512]{1,0:T(1,128)}, u32[]{:S(2)}) %copy-start.4) | copy-done | bytes 2072
  5.4 0.0 copy-start.5
  5.4 0.7 %copy-done.5 = s32[1,8]{1,0:T(1,128)S(1)} copy-done((s32[1,8]{1,0:T(1,128)S(1)}, s32[1,8]{1,0:T(1,128)}, u32[]{:S(2)}) %copy-start.5) | copy-done | bytes 56
  6.1 48.9 %shard_map.77 = (f32[1,256,1024]{2,1,0:T(8,128)S(1)}, f32[1,256,1024]{2,1,0:T(8,128)S(1)}) custom-call(bf16[1024,512]{1,0:T(8,128)(2,1)S(1)} %copy-done, bf16[8,3,128,128]{3,2,1,0:T(8,128)(2,1)S(1)} %copy-done.1, f32[1,512]{1,0:T(1,128)S(1)} %copy-done.3, s32[1,512]{1,0:T(1,128)S(1)} %copy-done.4, f32[1,8,128,128]{3,2,1,0:T(8,128)S(1)} %copy-done.2, ...), custom_call_target="tpu_custom_call" | custom-call | tf_op jit(solution)/shard_map/pallas_call | solution.py:387
  54.9 1.0 %copy.10 = f32[1,256,1024]{2,1,0:T(8,128)} copy(f32[1,256,1024]{2,1,0:T(8,128)S(1)} %get-tuple-element.4) | data formatting | bytes 2097152
  55.9 1.0 %copy.11 = f32[1,256,1024]{2,1,0:T(8,128)} copy(f32[1,256,1024]{2,1,0:T(8,128)S(1)} %get-tuple-element.5) | data formatting | bytes 2097152
Async XLA Ops:
  0.6 1.2 %copy-start = (bf16[1024,512]{1,0:T(8,128)(2,1)S(1)}, bf16[1024,512]{1,0:T(8,128)(2,1)}, u32[]{:S(2)}) copy-start(bf16[1024,512]{1,0:T(8,128)(2,1)} %anom.1) | copy-start | bytes 3145732
  1.9 1.1 %copy-start.1 = (bf16[8,3,128,128]{3,2,1,0:T(8,128)(2,1)S(1)}, bf16[8,3,128,128]{3,2,1,0:T(8,128)(2,1)}, u32[]{:S(2)}) copy-start(bf16[8,3,128,128]{3,2,1,0:T(8,128)(2,1)} %local.1) | copy-start | bytes 2359300
  3.0 1.0 %copy-start.2 = (f32[1,8,128,128]{3,2,1,0:T(8,128)S(1)}, f32[1,8,128,128]{3,2,1,0:T(8,128)}, u32[]{:S(2)}) copy-start(f32[1,8,128,128]{3,2,1,0:T(8,128)} %tangent.1) | copy-start | bytes 1572868
  4.0 0.7 %copy-start.3 = (f32[1,512]{1,0:T(1,128)S(1)}, f32[1,512]{1,0:T(1,128)}, u32[]{:S(2)}) copy-start(f32[1,512]{1,0:T(1,128)} %innov.1) | copy-start | bytes 6148
  4.7 0.7 %copy-start.4 = (s32[1,512]{1,0:T(1,128)S(1)}, s32[1,512]{1,0:T(1,128)}, u32[]{:S(2)}) copy-start(s32[1,512]{1,0:T(1,128)} %obs.1) | copy-start | bytes 6148
  5.4 0.7 %copy-start.5 = (s32[1,8]{1,0:T(1,128)S(1)}, s32[1,8]{1,0:T(1,128)}, u32[]{:S(2)}) copy-start(s32[1,8]{1,0:T(1,128)} %order.1) | copy-start | bytes 100

commit v2 on v1

--- a/solution.py
+++ b/solution.py
@@ -24,14 +24,21 @@
 
 def kernel(
     dims,
+    anom_h,
+    local_h,
+    innov_h,
+    obs_h,
+    tangent_h,
+    order_h,
+    fwd_out,
+    adj_out,
     anom,
     local,
     innov,
     obs,
     tangent,
     order,
-    fwd_out,
-    adj_out,
+    load_sem,
     other,
     halo,
     halo_innov,
@@ -67,6 +74,21 @@
     a_recv,
 ):
     n_tm, n_lon, n_ens, rows, chunk = dims
+    loads = [
+        pltpu.make_async_copy(src, dst, load_sem.at[i])
+        for i, (src, dst) in enumerate(
+            (
+                (innov_h, innov),
+                (obs_h, obs),
+                (anom_h, anom),
+                (local_h, local),
+                (tangent_h, tangent),
+                (order_h, order),
+            )
+        )
+    ]
+    for load in loads:
+        load.start()
     cells, cols = anom.shape
     n_blocks = cells // BLK
     n_pieces = tangent.shape[1]
@@ -122,21 +144,21 @@
 
     edge = pl.ds(pl.multiple_of((1 - parity) * (cells - BLK), BLK), BLK)
     toward = jnp.where(parity == 0, right, left)
-    halo_copy = remote(anom.at[edge], halo.at[parity], h_send.at[0], h_recv.at[0], at(ll=toward))
+    halo_copy = remote(anom_h.at[edge], halo.at[parity], h_send.at[0], h_recv.at[0], at(ll=toward))
     halo_copy.start()
     obs_copies = []
     for side, where in ((0, right), (1, left)):
         obs_copies.append(
-            remote(innov, halo_innov.at[side], o_send.at[side], o_recv.at[side], at(ll=where))
+            remote(innov_h, halo_innov.at[side], o_send.at[side], o_recv.at[side], at(ll=where))
         )
         obs_copies.append(
-            remote(obs, halo_obs.at[side], o_send.at[2 + side], o_recv.at[2 + side], at(ll=where))
+            remote(obs_h, halo_obs.at[side], o_send.at[2 + side], o_recv.at[2 + side], at(ll=where))
         )
     for copy in obs_copies:
         copy.start()
     x_copies = [
         [
-            x_copy(d, s, x_send, x_recv, at(ee=lax.rem(e + d, n_ens)), anom)
+            x_copy(d, s, x_send, x_recv, at(ee=lax.rem(e + d, n_ens)), anom_h)
             for s in range(SUBS)
         ]
         for d in range(1, n_ens)
@@ -145,6 +167,8 @@
         for d in range(1, n_ens):
             x_copies[d - 1][s].start()
 
+    for load in loads[:3]:
+        load.wait()
     innov_row, obs_row = innov[...], obs[...]
 
     def weigh(b, _):
@@ -166,6 +190,7 @@
         localize(b)
         return 0
 
+    loads[3].wait()
     lax.fori_loop(1, n_blocks - 1, inner, 0)
 
     halo_copy.wait_recv()
@@ -184,6 +209,8 @@
         map_f[i, BLK : 2 * BLK, :] = (turned - high.astype(F32)).astype(BF16)
         return 0
 
+    loads[4].wait()
+    loads[5].wait()
     lax.fori_loop(0, n_pieces, split_map, 0)
 
     for copy in obs_copies:
@@ -387,9 +414,16 @@
     return pl.pallas_call(
         functools.partial(kernel, (n_tm, n_lon, n_ens, rows, chunk)),
         out_shape=(out, out),
-        in_specs=[in_vmem] * 5 + [pl.BlockSpec(memory_space=pltpu.SMEM)],
+        in_specs=[pl.BlockSpec(memory_space=pl.ANY)] * 6,
         out_specs=(in_vmem, in_vmem),
         scratch_shapes=[
+            vmem(anomalies.shape, BF16),
+            vmem(localization.shape, BF16),
+            vmem(innovations.shape, F32),
+            vmem(obs_cell.shape, jnp.int32),
+            vmem(tangent_blocks.shape, F32),
+            pltpu.SMEM(tangent_order.shape, jnp.int32),
+            dma((6,)),
             vmem((max(n_ens - 1, 1), cells, cols), BF16),
             vmem((2, BLK, cols), BF16),
             vmem((2, 1, obs), F32),
@@ -425,7 +459,7 @@
             dma((n_chunks,)),
         ],
         compiler_params=pltpu.CompilerParams(
-            collective_id=0, has_side_effects=True, vmem_limit_bytes=40 * 1024 * 1024
+            collective_id=0, has_side_effects=True, vmem_limit_bytes=56 * 1024 * 1024
         ),
     )(anomalies, localization, innovations, obs_cell, tangent_blocks, tangent_order)
 

time: 57.2 us -> 54.1 us (0.946)
  local copies, waits for them, and re-layouts: 7.35 us -> 3.37 us
  Pallas kernels: 48.9 us -> 50 us
    unnamed x14 -> x4, local copies, waits for them, and re-layouts: 7.35 us -> 3.37 us
    pallas_call x1, Pallas kernels: 48.9 us -> 50 us  [on_device(): pl.pallas_call(functools.partial(kernel, (n_tm, n_lon, n_ens, rows, chunk...]
where the time goes in v2:
time: 54.1 us; the launch traced here: 54 us
  Pallas kernels  50 us (92%)
  local copies, waits for them, and re-layouts  3.37 us (6%)
  between operations  0.65 us (1%)
    pallas_call x1, Pallas kernels, on_device(): pl.pallas_call(functools.partial(kernel, (n_tm, n_lon, n_ens, rows, chunk...  50 us
    unnamed x4, local copies, waits for them, and re-layouts  3.37 us

profile of v2, /device:TPU:0, one launch (start us, length us, event | category | flops | bytes accessed | tf_op | source)
XLA Modules:
  0.0 54.0 jit_solution(3103232253260147723)
XLA Ops:
  0.6 50.0 %shard_map.77 = (f32[1,256,1024]{2,1,0:T(8,128)}, f32[1,256,1024]{2,1,0:T(8,128)}) custom-call(bf16[1024,512]{1,0:T(8,128)(2,1)} %anom_h.1, bf16[8,3,128,128]{3,2,1,0:T(8,128)(2,1)} %local_h.1, f32[1,512]{1,0:T(1,128)} %innov_h.1, s32[1,512]{1,0:T(1,128)} %obs_h.1, f32[1,8,128,128]{3,2,1,0:T(8,128)} %tangent_h.1, s32[1,8]{1,0:T(1,128)} %order_h.1), custom_call_target="tpu_custom_call" | custom-call | tf_op jit(solution)/shard_map/pallas_call | solution.py:414
  50.6 0.0 copy-start
  50.6 2.4 %copy.10 = f32[1,256,1024]{2,1,0:T(8,128)} copy(f32[1,256,1024]{2,1,0:T(8,128)} %get-tuple-element.4) | data formatting | bytes 2097152
  53.0 0.0 copy-done
  53.0 1.0 %copy.11 = f32[1,256,1024]{2,1,0:T(8,128)} copy(f32[1,256,1024]{2,1,0:T(8,128)S(1)} %copy-done) | data formatting | bytes 2097152
Async XLA Ops:
  50.6 2.4 %copy-start = (f32[1,256,1024]{2,1,0:T(8,128)S(1)}, f32[1,256,1024]{2,1,0:T(8,128)}, u32[]{:S(2)}) copy-start(f32[1,256,1024]{2,1,0:T(8,128)} %get-tuple-element.5) | copy-start | bytes 3145732

commit v3 on v2

--- a/solution.py
+++ b/solution.py
@@ -9,6 +9,7 @@
 
 BLK = 128
 SUBS = 4
+LAG = 4
 F32 = jnp.float32
 BF16 = jnp.bfloat16
 
@@ -351,7 +352,7 @@
         def _():
             gather_force(s)
 
-        c_f = s - t
+        c_f = s - LAG * t
 
         @pl.when((c_f >= 0) & (c_f < n_chunks))
         def _():
@@ -361,7 +362,7 @@
         def _():
             apply_force(s)
 
-        c_a = s - (n_tm - 1 - t)
+        c_a = s - LAG * (n_tm - 1 - t)
 
         @pl.when((c_a >= 0) & (c_a < n_chunks))
         def _():
@@ -369,7 +370,7 @@
 
         return 0
 
-    lax.fori_loop(0, n_tm - 1 + n_chunks, turn, 0)
+    lax.fori_loop(0, LAG * (n_tm - 1) + n_chunks, turn, 0)
 
     halo_copy.wait_send()
     halo_mate.wait_send()
@@ -399,7 +400,7 @@
     cells, cols = anomalies.shape
     rank = cols * n_ens
     rows = cols // n_lon
-    chunk = min(64, rows)
+    chunk = min(32, rows)
     n_chunks = rows // chunk
     pieces = tangent_blocks.shape[1]
     obs = innovations.shape[1]

time: 54.1 us -> 49.3 us (0.911)
  Pallas kernels: 50 us -> 45.2 us
    pallas_call x1, Pallas kernels: 50 us -> 45.2 us  [on_device(): pl.pallas_call(functools.partial(kernel, (n_tm, n_lon, n_ens, rows, chunk...]
where the time goes in v3:
time: 49.3 us; the launch traced here: 49.2 us
  Pallas kernels  45.2 us (92%)
  local copies, waits for them, and re-layouts  3.37 us (7%)
  between operations  0.65 us (1%)
    pallas_call x1, Pallas kernels, on_device(): pl.pallas_call(functools.partial(kernel, (n_tm, n_lon, n_ens, rows, chunk...  45.2 us
    unnamed x4, local copies, waits for them, and re-layouts  3.37 us

profile of v3, /device:TPU:0, one launch (start us, length us, event | category | flops | bytes accessed | tf_op | source)
XLA Modules:
  0.0 49.2 jit_solution(4722849046126383332)
XLA Ops:
  0.6 45.2 %shard_map.77 = (f32[1,256,1024]{2,1,0:T(8,128)}, f32[1,256,1024]{2,1,0:T(8,128)}) custom-call(bf16[1024,512]{1,0:T(8,128)(2,1)} %anom_h.1, bf16[8,3,128,128]{3,2,1,0:T(8,128)(2,1)} %local_h.1, f32[1,512]{1,0:T(1,128)} %innov_h.1, s32[1,512]{1,0:T(1,128)} %obs_h.1, f32[1,8,128,128]{3,2,1,0:T(8,128)} %tangent_h.1, s32[1,8]{1,0:T(1,128)} %order_h.1), custom_call_target="tpu_custom_call" | custom-call | tf_op jit(solution)/shard_map/pallas_call | solution.py:415
  45.8 0.0 copy-start
  45.8 2.4 %copy.10 = f32[1,256,1024]{2,1,0:T(8,128)} copy(f32[1,256,1024]{2,1,0:T(8,128)} %get-tuple-element.4) | data formatting | bytes 2097152
  48.2 0.0 copy-done
  48.2 1.0 %copy.11 = f32[1,256,1024]{2,1,0:T(8,128)} copy(f32[1,256,1024]{2,1,0:T(8,128)S(1)} %copy-done) | data formatting | bytes 2097152
Async XLA Ops:
  45.8 2.4 %copy-start = (f32[1,256,1024]{2,1,0:T(8,128)S(1)}, f32[1,256,1024]{2,1,0:T(8,128)}, u32[]{:S(2)}) copy-start(f32[1,256,1024]{2,1,0:T(8,128)} %get-tuple-element.5) | copy-start | bytes 3145732

commit v4 on v3

--- a/solution.py
+++ b/solution.py
@@ -10,6 +10,7 @@
 BLK = 128
 SUBS = 4
 LAG = 4
+STORES = 4
 F32 = jnp.float32
 BF16 = jnp.bfloat16
 
@@ -395,6 +396,21 @@
             a_copy(c).wait_send()
 
 
+def store(fwd, adj, fwd_out, adj_out, sem):
+    part = fwd.shape[1] // STORES
+    copies = []
+    for which, (src, dst) in enumerate(((fwd, fwd_out), (adj, adj_out))):
+        for i in range(STORES):
+            span = pl.ds(i * part, part)
+            copies.append(
+                pltpu.make_async_copy(src.at[0, span], dst.at[0, span], sem.at[which, i])
+            )
+    for copy in copies:
+        copy.start()
+    for copy in copies:
+        copy.wait()
+
+
 def on_device(mesh_dims, anomalies, localization, innovations, obs_cell, tangent_blocks, tangent_order):
     n_tm, n_lon, n_ens = mesh_dims
     cells, cols = anomalies.shape
@@ -412,7 +428,7 @@
     x_sems = (max(n_ens - 1, 1), SUBS)
     in_vmem = pl.BlockSpec(memory_space=pltpu.VMEM)
     out = jax.ShapeDtypeStruct((1, rows, rank), F32)
-    return pl.pallas_call(
+    states = pl.pallas_call(
         functools.partial(kernel, (n_tm, n_lon, n_ens, rows, chunk)),
         out_shape=(out, out),
         in_specs=[pl.BlockSpec(memory_space=pl.ANY)] * 6,
@@ -463,6 +479,14 @@
             collective_id=0, has_side_effects=True, vmem_limit_bytes=56 * 1024 * 1024
         ),
     )(anomalies, localization, innovations, obs_cell, tangent_blocks, tangent_order)
+    return pl.pallas_call(
+        store,
+        out_shape=(out, out),
+        in_specs=[in_vmem] * 2,
+        out_specs=[pl.BlockSpec(memory_space=pl.ANY)] * 2,
+        scratch_shapes=[dma((2, STORES))],
+        compiler_params=pltpu.CompilerParams(vmem_limit_bytes=56 * 1024 * 1024),
+    )(*states)
 
 
 def solution(mesh):

time: 49.3 us -> 48.9 us (level)
  local copies, waits for them, and re-layouts: 3.37 us -> 0 us
  Pallas kernels: 45.2 us -> 48.1 us
    unnamed x4 -> x0, local copies, waits for them, and re-layouts: 3.37 us -> none
    pallas_call x0 -> x1, Pallas kernels: none -> 2.92 us  [on_device(): pl.pallas_call(store, out_shape=(out, out), in_specs=[in_vmem] * 2, out_s...]
where the time goes in v4:
time: 48.9 us; the launch traced here: 48.7 us
  Pallas kernels  48.1 us (98%)
  between operations  0.64 us (1%)
    pallas_call x1, Pallas kernels, on_device(): pl.pallas_call(functools.partial(kernel, (n_tm, n_lon, n_ens, rows, chunk...  45.2 us
    pallas_call x1, Pallas kernels, on_device(): pl.pallas_call(store, out_shape=(out, out), in_specs=[in_vmem] * 2, out_s...  2.92 us

profile of v4, /device:TPU:0, one launch (start us, length us, event | category | flops | bytes accessed | tf_op | source)
XLA Modules:
  0.0 48.7 jit_solution(10332957179682644491)
XLA Ops:
  0.6 45.2 %shard_map.77 = (f32[1,256,1024]{2,1,0:T(8,128)}, f32[1,256,1024]{2,1,0:T(8,128)}) custom-call(bf16[1024,512]{1,0:T(8,128)(2,1)} %anom_h.1, bf16[8,3,128,128]{3,2,1,0:T(8,128)(2,1)} %local_h.1, f32[1,512]{1,0:T(1,128)} %innov_h.1, s32[1,512]{1,0:T(1,128)} %obs_h.1, f32[1,8,128,128]{3,2,1,0:T(8,128)} %tangent_h.1, s32[1,8]{1,0:T(1,128)} %order_h.1), custom_call_target="tpu_custom_call" | custom-call | tf_op jit(solution)/shard_map/pallas_call | solution.py:431
  45.8 2.9 %shard_map.78 = (f32[1,256,1024]{2,1,0:T(8,128)}, f32[1,256,1024]{2,1,0:T(8,128)}) custom-call(f32[1,256,1024]{2,1,0:T(8,128)} %get-tuple-element.4.fwd, f32[1,256,1024]{2,1,0:T(8,128)} %get-tuple-element.5.adj), custom_call_target="tpu_custom_call" | custom-call | tf_op jit(solution)/shard_map/pallas_call | solution.py:482
